TPU v7x, 32 devices: a whole 2x2x4 slice. The times are simulated.
32 devices in a mesh: lon: 4 (over y, x), lat: 4 (over z), head: 2 (over core).
Axes of the slice: x: 2, y: 2, z: 4, core: 2. Of those that a mesh axis runs over, the one named last changes fastest.
Arguments:
- tokens: bfloat16 [32, 64, 1024], P('lat', 'lon'), may hold values from -60 to 60, as said below
- cotangent: bfloat16 [32, 64, 1024], P('lat', 'lon'), may hold values from -6 to 6
- w_qkv: bfloat16 [3, 1024, 1024], P(None, None, 'head'), may hold values from -0.1875 to 0.1875
- w_out: bfloat16 [1024, 1024], P('head'), may hold values from -0.1875 to 0.1875
- norm_gain: float32 [1024], replicated, may hold values from 0.1 to 1.9
- type_bias: float32 [3, 16], P(None, 'head'), may hold values from -310 to 310
- offsets: int32 [2], replicated, may hold values from 1 to 7
- window_kind: int32 [4, 8], replicated, may hold values from 0 to 2
Outputs:
- d_tokens: bfloat16 [32, 64, 1024], P('lat', 'lon')
Inputs may be any that keep to these rules, and one draw needn't show every extreme that they name: `tokens`: activations of order one with scales that differ between cells and between features.
All inputs are finite; a program needn't handle non-finite values.
Results may differ from a plain program's by a relative error of at most 0.011.
Values may be sent and summed in bfloat16 or wider, within the bound.
A program may use at most 64 MiB of HBM per device.

v0:
```python
import jax
import jax.numpy as jnp
from jax import lax
from jax.sharding import PartitionSpec as P

WIN = 8


epsilon = 1e-06


def extended(cells, sides, width, closed):
    for axis, dim in sides:
        count = lax.axis_size(axis)
        ends = count if closed else count - 1
        head = lax.slice_in_dim(cells, 0, width, axis=dim)
        tail = lax.slice_in_dim(cells, cells.shape[dim] - width, cells.shape[dim], axis=dim)
        cells = jnp.concatenate(
            [
                lax.ppermute(tail, axis, [(i, (i + 1) % count) for i in range(ends)]),
                cells,
                lax.ppermute(head, axis, [((i + 1) % count, i) for i in range(ends)]),
            ],
            axis=dim,
        )
    return cells


def normalize(cells, gains):
    cells_f32 = cells.astype(jnp.float32)
    inverse_rms = lax.rsqrt(jnp.mean(cells_f32 * cells_f32, axis=-1, keepdims=True) + epsilon)
    return ((cells_f32 * inverse_rms * gains).astype(jnp.bfloat16), cells_f32, inverse_rms)


def norm_back(cells_f32, inverse_rms, gains, d_normed):
    scaled = d_normed * gains
    row_inner = jnp.mean(cells_f32 * scaled, axis=-1, keepdims=True)
    return inverse_rms * scaled - cells_f32 * (inverse_rms * inverse_rms * inverse_rms) * row_inner


def attend_back(q_heads, k_heads, v_heads, d_heads, key_bias, allowed, scale_val):
    logits = (
        jnp.einsum("wqhe,wkhe->whqk", q_heads, k_heads, preferred_element_type=jnp.float32)
        * scale_val
    )
    logits = logits + jnp.transpose(key_bias, (0, 2, 1))[:, :, None, :]
    logits = jnp.where(allowed[:, None], logits, -jnp.inf)
    peak_val = jnp.max(logits, axis=-1, keepdims=True)
    expo_val = jnp.exp(logits - peak_val)
    weights = expo_val / jnp.sum(expo_val, axis=-1, keepdims=True)
    weights_low = weights.astype(jnp.bfloat16)
    d_values = jnp.einsum(
        "whqk,wqhe->wkhe", weights_low, d_heads, preferred_element_type=jnp.float32
    ).astype(jnp.bfloat16)
    d_weights = jnp.einsum("wqhe,wkhe->whqk", d_heads, v_heads, preferred_element_type=jnp.float32)
    row_inner = jnp.sum(weights * d_weights, axis=-1, keepdims=True)
    d_logits = (scale_val * weights * (d_weights - row_inner)).astype(jnp.bfloat16)
    d_queries = jnp.einsum(
        "whqk,wkhe->wqhe", d_logits, k_heads, preferred_element_type=jnp.float32
    ).astype(jnp.bfloat16)
    d_keys = jnp.einsum(
        "whqk,wqhe->wkhe", d_logits, q_heads, preferred_element_type=jnp.float32
    ).astype(jnp.bfloat16)
    return (d_queries, d_keys, d_values)


def to_windows(grid):
    row_count, col_count = (grid.shape[0], grid.shape[1])
    grid = grid.reshape((row_count // WIN, WIN, col_count // WIN, WIN) + grid.shape[2:])
    grid = jnp.moveaxis(grid, 2, 1)
    return grid.reshape((row_count // WIN * (col_count // WIN), WIN * WIN) + grid.shape[4:])


def from_windows(flat, row_count, col_count):
    grid = flat.reshape((row_count // WIN, col_count // WIN, WIN, WIN) + flat.shape[2:])
    grid = jnp.moveaxis(grid, 1, 2)
    return grid.reshape((row_count, col_count) + flat.shape[2:])


def on_device(tokens, cotangent, w_qkv, w_out, norm_gain, type_bias, offsets, window_kind):
    tile_rows, tile_cols, model_width = tokens.shape
    local_width = w_out.shape[0]
    head_count = type_bias.shape[1]
    head_dim = local_width // head_count
    rim_width = WIN - 1
    row_shift = offsets[0]
    col_shift = offsets[1]
    region_rows = tile_rows + WIN
    region_cols = tile_cols + WIN
    total_rows = tile_rows * lax.axis_size("lat")
    total_cols = tile_cols * lax.axis_size("lon")
    normed_own, cells_own, inverse_own = normalize(tokens, norm_gain)
    stacked = jnp.concatenate([tokens, cotangent], axis=-1)
    tall_ext = extended(stacked, (("lat", 0),), rim_width, False)
    full_ext = extended(tall_ext, (("lon", 1),), rim_width, True)
    region = lax.dynamic_slice(
        full_ext, (row_shift - 1, col_shift - 1, 0), (region_rows, region_cols, 2 * model_width)
    )
    region_normed = normalize(region[:, :, :model_width], norm_gain)[0]
    proj = jnp.einsum(
        "rcd,kde->rcke", region_normed, w_qkv, preferred_element_type=jnp.float32
    ).astype(jnp.bfloat16)
    d_grid = jnp.einsum(
        "rcd,ed->rce", region[:, :, model_width:], w_out, preferred_element_type=jnp.float32
    ).astype(jnp.bfloat16)
    glob_rows = (
        lax.axis_index("lat") * tile_rows
        + row_shift
        - WIN
        + jnp.arange(region_rows, dtype=jnp.int32)
    )
    glob_cols = jnp.remainder(
        lax.axis_index("lon") * tile_cols
        + col_shift
        - WIN
        + jnp.arange(region_cols, dtype=jnp.int32),
        total_cols,
    )
    kind_rows = jnp.take(window_kind, jnp.remainder(glob_rows, total_rows) // WIN, axis=0)
    kind_grid = jnp.take(kind_rows, glob_cols // WIN, axis=1)
    one_hot = (kind_grid[:, :, None] == jnp.arange(3, dtype=jnp.int32)).astype(jnp.float32)
    cell_bias = jnp.einsum("rck,kh->rch", one_hot, type_bias, precision=lax.Precision.HIGHEST)
    seam_side = jnp.floor_divide(glob_rows, total_rows)
    side_grid = jnp.broadcast_to(seam_side[:, None], (region_rows, region_cols))
    side_windows = to_windows(side_grid)
    allowed = side_windows[:, :, None] == side_windows[:, None, :]
    proj_windows = to_windows(proj)
    window_count = proj_windows.shape[0]
    head_shape = (window_count, WIN * WIN, head_count, head_dim)
    q_heads = proj_windows[:, :, 0].reshape(head_shape)
    k_heads = proj_windows[:, :, 1].reshape(head_shape)
    v_heads = proj_windows[:, :, 2].reshape(head_shape)
    d_heads = to_windows(d_grid).reshape(head_shape)
    d_queries, d_keys, d_values = attend_back(
        q_heads, k_heads, v_heads, d_heads, to_windows(cell_bias), allowed, head_dim ** (-0.5)
    )
    d_all = jnp.stack([d_queries, d_keys, d_values], axis=2).reshape(
        window_count, WIN * WIN, 3, local_width
    )
    d_region = from_windows(d_all, region_rows, region_cols)
    d_owned = lax.dynamic_slice(
        d_region, (WIN - row_shift, WIN - col_shift, 0, 0), (tile_rows, tile_cols, 3, local_width)
    )
    d_part = jnp.einsum("rcke,kde->rcd", d_owned, w_qkv, preferred_element_type=jnp.float32)
    d_normed = lax.psum(d_part, "head")
    result = (
        cotangent.astype(jnp.float32) + norm_back(cells_own, inverse_own, norm_gain, d_normed)
    ).astype(jnp.bfloat16)
    return result


def solution(mesh):
    return jax.shard_map(
        on_device,
        mesh=mesh,
        in_specs=(
            P("lat", "lon", None),
            P("lat", "lon", None),
            P(None, None, "head"),
            P("head", None),
            P(),
            P(None, "head"),
            P(),
            P(),
        ),
        out_specs=P("lat", "lon", None),
        check_vma=False,
    )
```

profile of v0, /device:TPU:9, one launch (start us, length us, event | category | flops | bytes accessed | tf_op | source)
XLA Modules:
  0.0 143.8 jit_solution(5061777898060464719)
XLA Ops:
  10.5 1.9 %collective-permute-start.1 = (bf16[7,16,2048]{2,1,0:T(8,128)(2,1)}, bf16[7,16,2048]{2,1,0:T(8,128)(2,1)}, u32[]{:S(2)}, u32[]{:S(2)}) collective-permute-start(bf16[7,16,2048]{2,1,0:T(8,128)(2,1)} %get-tuple-element.13), channel_id=1, source_target_pairs={{2,0},{4,2},{6,4},{3,1},{5,3},{7,5},{10,8},{12,10},{14,12},{11,9},... | collective-permute-start | bytes 1376264 | tf_op jit(solution)/shard_map/ppermute | solution.py:22
  12.4 3.4 %collective-permute-start = (bf16[7,16,2048]{2,1,0:T(8,128)(2,1)}, bf16[7,16,2048]{2,1,0:T(8,128)(2,1)}, u32[]{:S(2)}, u32[]{:S(2)}) collective-permute-start(bf16[7,16,2048]{2,1,0:T(8,128)(2,1)} %get-tuple-element.12), channel_id=1, source_target_pairs={{0,2},{2,4},{4,6},{1,3},{3,5},{5,7},{8,10},{10,12},{12,14},{9,11},... | collective-permute-start | bytes 1376264 | tf_op jit(solution)/shard_map/ppermute | solution.py:20
  19.2 4.9 %collective-permute-done.1 = bf16[7,16,2048]{2,1,0:T(8,128)(2,1)} collective-permute-done((bf16[7,16,2048]{2,1,0:T(8,128)(2,1)}, bf16[7,16,2048]{2,1,0:T(8,128)(2,1)}, u32[]{:S(2)}, u32[]{:S(2)}) %collective-permute-start.1) | collective-permute-done | bytes 458784 | tf_op jit(solution)/shard_map/ppermute | solution.py:22
  24.1 1.9 %collective-permute-done = bf16[7,16,2048]{2,1,0:T(8,128)(2,1)} collective-permute-done((bf16[7,16,2048]{2,1,0:T(8,128)(2,1)}, bf16[7,16,2048]{2,1,0:T(8,128)(2,1)}, u32[]{:S(2)}, u32[]{:S(2)}) %collective-permute-start) | collective-permute-done | bytes 458784 | tf_op jit(solution)/shard_map/ppermute | solution.py:20
  40.0 5.6 %collective-permute-done.2 = bf16[22,7,2048]{2,0,1:T(8,128)(2,1)} collective-permute-done((bf16[22,7,2048]{2,0,1:T(8,128)(2,1)}, bf16[22,7,2048]{2,0,1:T(8,128)(2,1)}, u32[]{:S(2)}, u32[]{:S(2)}) %collective-permute-start.2) | collective-permute-done | bytes 630816 | tf_op jit(solution)/shard_map/ppermute | solution.py:20
  47.0 12.9 %collective-permute-done.3 = bf16[22,7,2048]{2,0,1:T(8,128)(2,1)} collective-permute-done((bf16[22,7,2048]{2,0,1:T(8,128)(2,1)}, bf16[22,7,2048]{2,0,1:T(8,128)(2,1)}, u32[]{:S(2)}, u32[]{:S(2)}) %collective-permute-start.3) | collective-permute-done | bytes 630816 | tf_op jit(solution)/shard_map/ppermute | solution.py:22
  61.4 4.1 %fusion.10 = bf16[16,24,2048]{2,1,0:T(8,128)(2,1)S(1)} fusion(s32[]{:T(128)S(6)} %select_n.132, s32[]{:T(128)S(6)} %select_n.133, bf16[22,7,2048]{2,1,0:T(8,128)(2,1)S(1)} %copy.61, bf16[7,16,2048]{2,1,0:T(8,128)(2,1)} %collective-permute-done, bf16[8,16,2048]{2,1,0:T(8,128)(2,1)S(1)} %copy-done.2, bf16[7,16,2048]{2,1,0:T(8,128)(2,1)} %collective-permute-done.1, ...), kind=kLoop, calls=%fused_computation.19 | loop fusion | flops 7864320 | bytes 4276232 | tf_op jit(solution)/shard_map/concatenate | solution.py:18
  68.0 2.4 %copy.79 = bf16[6,64,8,64]{1,3,2,0:T(8,128)(2,1)} copy(bf16[6,64,8,64]{3,2,1,0:T(8,128)(2,1)} %reshape_reshape.4) | data formatting | bytes 786432 | tf_op jit(solution)/shard_map/reshape;reshape | solution.py:133
  70.4 2.6 %fusion.13 = bf16[16,24,3,512]{3,1,2,0:T(8,128)(2,1)S(1)} fusion(bf16[3,1024,512]{2,1,0:T(8,128)(2,1)S(1)} %copy-done, f32[1024]{0:T(1024)S(1)} %copy-done.11, f32[16,24]{1,0:T(8,128)S(1)} %add_rsqrt_fusion, bf16[16,24,2048]{2,1,0:T(8,128)(2,1)} %copy-done.7), kind=kOutput, calls=%fused_computation.25 | convolution fusion | flops 1210122240 | bytes 5117440 | tf_op jit(solution)/shard_map/rcd,kde->rcke/dot_general | solution.py:100
  74.1 2.2 %copy.91 = bf16[6,64,1,512]{1,3,0,2:T(8,128)(2,1)} copy(bf16[6,64,1,512]{3,1,2,0:T(8,128)(2,1)} %get-tuple-element.10) | data formatting | bytes 786432 | tf_op jit(solution)/shard_map/reshape;squeeze | solution.py:130
  76.3 2.2 %copy.90 = bf16[6,64,1,512]{1,3,0,2:T(8,128)(2,1)} copy(bf16[6,64,1,512]{3,1,2,0:T(8,128)(2,1)} %get-tuple-element.11) | data formatting | bytes 786432 | tf_op jit(solution)/shard_map/reshape;squeeze | solution.py:131
  78.4 2.1 %add_select_fusion = f32[6,8,64,64]{2,3,1,0:T(8,128)S(1)} fusion(bf16[6,64,8,64]{1,3,2,0:T(8,128)(2,1)} %bitcast.83, bf16[6,64,8,64]{1,3,2,0:T(8,128)(2,1)} %bitcast.85, f32[6,8,64]{2,1,0:T(8,128)} %bitcast.93, pred[6,64,64]{1,2,0:T(8,128)(4,1)} %broadcast_compare_fusion), kind=kOutput, calls=%fused_computation.24 | convolution fusion | flops 25755648 | bytes 1609728 | tf_op jit(solution)/shard_map/wqhe,wkhe->whqk/dot_general | solution.py:43
  80.6 2.2 %fusion.53 = (f32[6,8,64]{2,1,0:T(8,128)}, f32[6,8,64,64]{2,3,1,0:T(8,128)}) fusion(f32[6,8,64,64]{2,3,1,0:T(8,128)S(1)} %add_select_fusion), kind=kOutput, calls=%fused_computation.121 | output fusion | flops 393279 | bytes 1585152 | tf_op jit(solution)/shard_map/sub | solution.py:49
  84.1 3.6 %fusion.19 = bf16[6,64,8,64]{1,3,2,0:T(8,128)(2,1)} fusion(bf16[6,64,8,64]{1,3,2,0:T(8,128)(2,1)} %copy.79, f32[6,8,64]{2,1,0:T(8,128)} %get-tuple-element.18, f32[6,8,64,64]{2,3,1,0:T(8,128)} %copy-done.5), kind=kOutput, calls=%fused_computation.33 | convolution fusion | flops 25955392 | bytes 1585152 | tf_op jit(solution)/shard_map/whqk,wqhe->wkhe/dot_general | solution.py:52
  87.7 2.4 %multiply_reduce_fusion = (f32[6,8,64]{2,1,0:T(8,128)S(1)}, f32[6,8,64,64]{2,3,1,0:T(8,128)S(1)}) fusion(f32[6,8,64,64]{2,3,1,0:T(8,128)} %get-tuple-element.19, f32[6,8,64]{2,1,0:T(8,128)S(1)} %copy-done.10, bf16[6,64,8,64]{1,3,2,0:T(8,128)(2,1)} %copy.79, bf16[6,64,8,64]{3,2,1,0:T(8,128)(2,1)} %reshape_squeeze.11), kind=kOutput, calls=%fused_computation.23 | convolution fusion | flops 25752576 | bytes 2383872 | tf_op jit(solution)/shard_map/wqhe,wkhe->whqk/dot_general | solution.py:55
  94.0 2.4 %copy.81 = bf16[6,64,8,64]{3,2,1,0:T(8,128)(2,1)} copy(bf16[6,64,8,64]{1,3,2,0:T(8,128)(2,1)} %fusion.19) | data formatting | bytes 786432 | tf_op jit(solution)/shard_map/convert_element_type | solution.py:54
  96.4 1.7 %stack.14 = bf16[2,3,8,8,1,512]{5,3,2,1,0,4:T(8,128)(2,1)S(1)} reshape(bf16[6,64,8,64]{3,2,1,0:T(8,128)(2,1)} %copy.81) | data formatting | bytes 786432 | tf_op jit(solution)/shard_map/stack | solution.py:137
  98.1 2.4 %copy.78 = bf16[6,64,8,64]{3,2,1,0:T(8,128)(2,1)} copy(bf16[6,64,8,64]{1,3,2,0:T(8,128)(2,1)} %fusion.18) | data formatting | bytes 786432 | tf_op jit(solution)/shard_map/convert_element_type | solution.py:63
  100.5 2.4 %stack.13 = bf16[2,3,8,8,1,512]{5,3,2,1,0,4:T(8,128)(2,1)} reshape(bf16[6,64,8,64]{3,2,1,0:T(8,128)(2,1)} %copy.78) | data formatting | bytes 786432 | tf_op jit(solution)/shard_map/stack | solution.py:137
  102.9 2.4 %copy.75 = bf16[6,64,8,64]{3,2,1,0:T(8,128)(2,1)} copy(bf16[6,64,8,64]{1,3,2,0:T(8,128)(2,1)} %fusion.17) | data formatting | bytes 786432 | tf_op jit(solution)/shard_map/convert_element_type | solution.py:60
  105.3 2.3 %stack.12 = bf16[2,3,8,8,1,512]{5,3,2,1,0,4:T(8,128)(2,1)} reshape(bf16[6,64,8,64]{3,2,1,0:T(8,128)(2,1)} %copy.75) | data formatting | bytes 786432 | tf_op jit(solution)/shard_map/stack | solution.py:137
  109.0 1.9 %fusion.20 = f32[8,16,1024]{2,1,0:T(8,128)} fusion(bf16[3,1024,512]{2,1,0:T(8,128)(2,1)S(1)} %copy-done, bf16[16,24,3,512]{3,1,2,0:T(8,128)(2,1)S(1)} %bitcast.89, s32[]{:T(128)S(6)} %select_n.150, s32[]{:T(128)S(6)} %select_n.151), kind=kOutput, calls=%fused_computation.35 | convolution fusion | flops 402653184 | bytes 4063240 | tf_op jit(solution)/shard_map/rcke,kde->rcd/dot_general | solution.py:144
  111.0 22.7 %all-reduce.2.cloned.1.call-done = f32[8,16,1024]{2,1,0:T(8,128)} async-done(((f32[8,16,1024]{2,1,0:T(8,128)}), f32[8,16,1024]{2,1,0:T(8,128)}) %all-reduce.2.cloned.1.call-update) | async-done | bytes 524304 | tf_op jit(solution)/shard_map/psum | solution.py:145
  134.9 2.1 %fusion.37 = bf16[8,16,1024]{2,1,0:T(8,128)(2,1)} fusion(bf16[8,16,1024]{2,1,0:T(8,128)(2,1)S(1)} %copy-done.8, bf16[8,16,1024]{2,1,0:T(8,128)(2,1)} %param.9, f32[8,16,1024]{2,1,0:T(8,128)} %all-reduce.2.cloned.1.call-done, f32[8,16]{1,0:T(8,128)S(1)} %broadcast_multiply_fusion, f32[8,16]{1,0:T(8,128)S(1)} %get-tuple-element.15, f32[1024]{0:T(1024)S(1)} %copy-done.11, ...), kind=kLoop, calls=%fused_computation.54 | loop fusion | flops 1179648 | bytes 1316352 | tf_op jit(solution)/shard_map/convert_element_type | solution.py:148
  (81 shorter events, 29.0 us)
Async XLA Ops:
  6.5 63.8 %copy-start = (bf16[3,1024,512]{2,1,0:T(8,128)(2,1)S(1)}, bf16[3,1024,512]{2,1,0:T(8,128)(2,1)}, u32[]{:S(2)}) copy-start(bf16[3,1024,512]{2,1,0:T(8,128)(2,1)} %param.10) | copy-start | bytes 9437188
  6.5 9.3 %copy-start.13 = (s32[2]{0:T(128)S(1)}, s32[2]{0:T(128)}, u32[]{:S(2)}) copy-start(s32[2]{0:T(128)} %param.14) | copy-start | bytes 28
  6.5 11.2 %copy-start.9 = (s32[4,8]{1,0:T(4,128)S(1)}, s32[4,8]{1,0:T(4,128)}, u32[]{:S(2)}) copy-start(s32[4,8]{1,0:T(4,128)} %param.15) | copy-start | bytes 388
  6.5 127.1 %all-reduce.2.cloned.1.call-start = ((), (), s32[]{:S(2)}) async-start(), calls=%async_computation | async-start | bytes 1048576 | tf_op jit(solution)/shard_map/psum | solution.py:145
  8.6 0.8 copy-start.1
  10.5 13.6 %collective-permute-start.1 = (bf16[7,16,2048]{2,1,0:T(8,128)(2,1)}, bf16[7,16,2048]{2,1,0:T(8,128)(2,1)}, u32[]{:S(2)}, u32[]{:S(2)}) collective-permute-start(bf16[7,16,2048]{2,1,0:T(8,128)(2,1)} %get-tuple-element.13), channel_id=1, source_target_pairs={{2,0},{4,2},{6,4},{3,1},{5,3},{7,5},{10,8},{12,10},{14,12},{11,9},... | collective-permute-start | bytes 1376264 | tf_op jit(solution)/shard_map/ppermute | solution.py:22
  12.4 13.6 %collective-permute-start = (bf16[7,16,2048]{2,1,0:T(8,128)(2,1)}, bf16[7,16,2048]{2,1,0:T(8,128)(2,1)}, u32[]{:S(2)}, u32[]{:S(2)}) collective-permute-start(bf16[7,16,2048]{2,1,0:T(8,128)(2,1)} %get-tuple-element.12), channel_id=1, source_target_pairs={{0,2},{2,4},{4,6},{1,3},{3,5},{5,7},{8,10},{10,12},{12,14},{9,11},... | collective-permute-start | bytes 1376264 | tf_op jit(solution)/shard_map/ppermute | solution.py:20
  27.7 8.8 %copy-start.12 = (f32[3,8]{1,0:T(4,128)S(1)}, f32[3,8]{1,0:T(4,128)}, u32[]{:S(2)}) copy-start(f32[3,8]{1,0:T(4,128)} %param.13) | copy-start | bytes 292
  29.0 16.6 %collective-permute-start.2 = (bf16[22,7,2048]{2,0,1:T(8,128)(2,1)}, bf16[22,7,2048]{2,0,1:T(8,128)(2,1)}, u32[]{:S(2)}, u32[]{:S(2)}) collective-permute-start(bf16[22,7,2048]{2,0,1:T(8,128)(2,1)} %copy.59), channel_id=1, source_target_pairs={{0,8},{8,16},{16,24},{24,0},{1,9},{9,17},{17,25},{25,1},{2,10},{10... | collective-permute-start | bytes 1892360 | tf_op jit(solution)/shard_map/ppermute | solution.py:20
  31.3 28.6 %collective-permute-start.3 = (bf16[22,7,2048]{2,0,1:T(8,128)(2,1)}, bf16[22,7,2048]{2,0,1:T(8,128)(2,1)}, u32[]{:S(2)}, u32[]{:S(2)}) collective-permute-start(bf16[22,7,2048]{2,0,1:T(8,128)(2,1)} %copy.60), channel_id=1, source_target_pairs={{8,0},{16,8},{24,16},{0,24},{9,1},{17,9},{25,17},{1,25},{10,2},{18... | collective-permute-start | bytes 1892360 | tf_op jit(solution)/shard_map/ppermute | solution.py:22
  39.3 22.1 %copy-start.2 = (bf16[8,16,2048]{2,1,0:T(8,128)(2,1)S(1)}, bf16[8,16,2048]{2,1,0:T(8,128)(2,1)}, u32[]{:S(2)}) copy-start(bf16[8,16,2048]{2,1,0:T(8,128)(2,1)} %copy-done.1) | copy-start | bytes 1572868
  61.4 4.3 %copy-start.14 = (bf16[512,1024]{1,0:T(8,128)(2,1)S(1)}, bf16[512,1024]{1,0:T(8,128)(2,1)}, u32[]{:S(2)}) copy-start(bf16[512,1024]{1,0:T(8,128)(2,1)} %param.11) | copy-start | bytes 3145732
  65.5 1.1 copy-start.7
  66.6 3.7 %copy-start.11 = (f32[1024]{0:T(1024)S(1)}, f32[1024]{0:T(1024)}, u32[]{:S(2)}) copy-start(f32[1024]{0:T(1024)} %param.12) | copy-start | bytes 12292
  80.6 2.3 %copy-start.5 = (f32[6,8,64,64]{2,3,1,0:T(8,128)}, f32[6,8,64,64]{2,3,1,0:T(8,128)S(1)}, u32[]{:S(2)}) copy-start(f32[6,8,64,64]{2,3,1,0:T(8,128)S(1)} %add_select_fusion) | copy-start | bytes 2359300
  84.1 3.6 %copy-start.10 = (f32[6,8,64]{2,1,0:T(8,128)S(1)}, f32[6,8,64]{2,1,0:T(8,128)}, u32[]{:S(2)}) copy-start(f32[6,8,64]{2,1,0:T(8,128)} %get-tuple-element.18) | copy-start | bytes 36868
  87.7 2.5 %copy-start.6 = (f32[6,8,64,64]{2,3,1,0:T(8,128)S(1)}, f32[6,8,64,64]{2,3,1,0:T(8,128)}, u32[]{:S(2)}) copy-start(f32[6,8,64,64]{2,3,1,0:T(8,128)} %get-tuple-element.19) | copy-start | bytes 2359300
  90.2 1.1 copy-start.3
  91.3 1.4 %copy-start.4 = (bf16[6,64,1,512]{1,3,0,2:T(8,128)(2,1)S(1)}, bf16[6,64,1,512]{1,3,0,2:T(8,128)(2,1)}, u32[]{:S(2)}) copy-start(bf16[6,64,1,512]{1,3,0,2:T(8,128)(2,1)} %copy.90) | copy-start | bytes 1179652
  109.0 24.7 %copy-start.8 = (bf16[8,16,1024]{2,1,0:T(8,128)(2,1)S(1)}, bf16[8,16,1024]{2,1,0:T(8,128)(2,1)}, u32[]{:S(2)}) copy-start(bf16[8,16,1024]{2,1,0:T(8,128)(2,1)} %param.8) | copy-start | bytes 786436
Sparse Core Ops, SparseCore 0:
  111.1 22.5 all-reduce.1
where the time goes:
time: 146 us; the launch traced here: 144 us
  waiting for transfers between devices  48 us (33%)
  local copies, waits for them, and re-layouts  37.8 us (26%)
  between operations  20 us (14%)
  matrix products  16.3 us (11%)
  other arithmetic  14 us (10%)
  starting transfers between devices  7.64 us (5%)
    psum x1, waiting for transfers between devices, on_device(): d_normed = lax.psum(d_part, 'head')  22.7 us
    ppermute x2, waiting for transfers between devices, extended(): lax.ppermute(head, axis, [((i + 1) % count, i) for i in range(ends)])  17.8 us
    ppermute x2, waiting for transfers between devices, extended(): lax.ppermute(tail, axis, [(i, (i + 1) % count) for i in range(ends)])  7.51 us
    another operation x3, local copies, waits for them, and re-layouts, on_device(): jnp.stack([d_queries, d_keys, d_values], axis=2)  6.45 us
    concatenate x2, other arithmetic, extended(): jnp.concatenate([lax.ppermute(tail, axis, [(i, (i + 1) % count) for i in...  5.55 us
    ppermute x2, starting transfers between devices, extended(): lax.ppermute(tail, axis, [(i, (i + 1) % count) for i in range(ends)])  4.41 us
    another operation x2, local copies, waits for them, and re-layouts, on_device(): d_heads = to_windows(d_grid).reshape(head_shape)  3.68 us
    dot_general x1, matrix products, attend_back(): jnp.einsum('whqk,wqhe->wkhe', weights_low, d_heads, preferred_element_typ...  3.61 us
  transfers between devices with their start and end apart: 5, of which 5 were waited for; matrix products, arithmetic and copies ran while one was open for 5% of the time, Pallas kernels for 0%

commit v1 on v0

v1 whole, which is shorter than its diff:
```python
import functools

import jax
import jax.numpy as jnp
from jax import lax
from jax.experimental import pallas as pl
from jax.experimental.pallas import tpu as pltpu
from jax.sharding import PartitionSpec as P

WIN = 8
AREA = WIN * WIN
EPSILON = 1e-06
MESH = pl.DeviceIdType.MESH
F32 = jnp.float32
BF16 = jnp.bfloat16


def dot(lhs, rhs, lhs_dim, rhs_dim):
    return lax.dot_general(
        lhs, rhs, (((lhs_dim,), (rhs_dim,)), ((), ())), preferred_element_type=F32
    )


def iota(shape, dim):
    return lax.broadcasted_iota(jnp.int32, shape, dim)


def one_hot(equal):
    return jnp.where(equal, 1.0, 0.0).astype(BF16)


def window_place(flat, row_shift, col_shift):
    row = ((flat >> 3) & 7) + row_shift
    col = ((flat >> 6) << 3) + (flat & 7) + col_shift
    return row >> 3, col >> 3, ((row & 7) << 3) + (col & 7)


def kernel(
    sizes,
    off_ref,
    kind_ref,
    bias_ref,
    gain_ref,
    tok_ref,
    cot_ref,
    wq_hbm,
    wo_hbm,
    out_ref,
    cells,
    wq,
    wo,
    proj,
    d_proj,
    part_out,
    part_in,
    ret_out,
    ret_in,
    joined,
    load_sem,
    near_send,
    near_recv,
    fwd_send,
    fwd_recv,
    part_send,
    part_recv,
    ret_send,
    ret_recv,
    join_send,
    join_recv,
):
    lons, lats, heads = sizes
    lon, lat, head = lax.axis_index("lon"), lax.axis_index("lat"), lax.axis_index("head")
    count, model = tok_ref.shape
    width = wo_hbm.shape[0]
    left, right = lax.rem(lon + lons - 1, lons), lax.rem(lon + 1, lons)
    up, down = lax.rem(lat + lats - 1, lats), lax.rem(lat + 1, lats)
    mates = [lax.rem(head + step, heads) for step in range(1, heads)]

    load_q = pltpu.make_async_copy(wq_hbm, wq, load_sem.at[0])
    load_o = pltpu.make_async_copy(wo_hbm, wo, load_sem.at[1])
    load_q.start()
    load_o.start()

    barrier = pltpu.get_barrier_semaphore()
    partners = [
        {"lon": left},
        {"lon": right},
        {"lat": up},
        {"lat": down},
        {"lon": right, "lat": down},
        {"lon": left, "lat": up},
    ] + [{"head": mate} for mate in mates]
    for partner in partners:
        pl.semaphore_signal(barrier, inc=1, device_id=partner, device_id_type=MESH)

    gain = gain_ref[...]
    tok = tok_ref[...].astype(F32)
    inverse = lax.rsqrt(jnp.mean(tok * tok, axis=-1, keepdims=True) + EPSILON)
    normed = (tok * inverse * gain).astype(BF16)
    big, small = iota((count, count), 0), iota((count, count), 1)

    def natural(flat):
        return (((flat >> 3) & 7) << 4) + ((flat >> 6) << 3) + (flat & 7)

    to_blocks = one_hot(natural(big) == small)
    from_blocks = one_hot(natural(small) == big)
    cells[0:2, 0] = dot(to_blocks, normed, 1, 0).astype(BF16).reshape(2, AREA, model)
    cells[0:2, 1] = dot(to_blocks, cot_ref[...], 1, 0).astype(BF16).reshape(2, AREA, model)

    pl.semaphore_wait(barrier, len(partners))

    share = AREA // heads
    rows = pl.ds(pl.multiple_of(head * share, share), share)

    def near(source, target, slot, device):
        return pltpu.make_async_remote_copy(
            src_ref=cells.at[source, :, rows],
            dst_ref=cells.at[target, :, rows],
            send_sem=near_send.at[slot],
            recv_sem=near_recv.at[slot],
            device_id=device,
            device_id_type=MESH,
        )

    from_below = near(0, 3, 0, {"lat": up})
    from_right = near(0, 2, 1, {"lon": left})
    from_below_next = near(1, 4, 2, {"lat": up})
    from_corner = near(3, 5, 3, {"lon": left})
    from_below.start()
    from_right.start()
    from_below_next.start()

    forwards = []

    def forward(block, slot):
        for step, mate in enumerate(mates):
            copy = pltpu.make_async_remote_copy(
                src_ref=cells.at[block, :, rows],
                dst_ref=cells.at[block, :, rows],
                send_sem=fwd_send.at[slot, step],
                recv_sem=fwd_recv.at[slot, step],
                device_id={"head": mate},
                device_id_type=MESH,
            )
            copy.start()
            forwards.append(copy)

    row_shift, col_shift = off_ref[0], off_ref[1]
    place_r = window_place(iota((count, 6 * AREA), 0), row_shift, col_shift)
    gather = one_hot(
        ((place_r[0] * 3 + place_r[1]) << 6) + place_r[2] == iota((count, 6 * AREA), 1)
    )
    place_c = window_place(iota((6 * AREA, count), 1), row_shift, col_shift)
    scatter = one_hot(
        ((place_c[0] * 3 + place_c[1]) << 6) + place_c[2] == iota((6 * AREA, count), 0)
    )

    local_heads = bias_ref.shape[1]
    head_dim = width // local_heads
    scale = head_dim ** (-0.5)
    lane_head = iota((1, width), 1) // head_dim
    kind_bias = []
    for kind in range(3):
        line = jnp.zeros((1, width), F32)
        for index in range(local_heads):
            line = jnp.where(lane_head == index, bias_ref[kind, index], line)
        kind_bias.append(line)
    group = min(width, 256)
    per_group = group // head_dim
    block_mask = one_hot(
        iota((group, group), 0) // head_dim == iota((group, group), 1) // head_dim
    )
    group_head = iota((1, group), 1) // head_dim
    query_row = (iota((AREA, group), 1) >> 3) & 7
    key_row = iota((AREA, group), 0) >> 3
    edge = lats * WIN - lat * WIN - row_shift
    allowed = (key_row >= edge) == (query_row >= edge)

    from_right.wait_recv()
    forward(2, 1)
    from_below.wait_recv()
    from_corner.start()
    forward(3, 0)
    from_below_next.wait_recv()
    forward(4, 2)
    load_q.wait()
    load_o.wait()
    from_corner.wait_recv()
    forward(5, 3)
    for copy in forwards:
        copy.wait_recv()

    picked = dot(gather, cells[:, 0].reshape(6 * AREA, model), 1, 0).astype(BF16)
    picked_cot = dot(gather, cells[:, 1].reshape(6 * AREA, model), 1, 0).astype(BF16)
    for index in range(3):
        proj[index] = dot(picked, wq[index], 1, 0).astype(BF16)
    proj[3] = dot(picked_cot, wo[...], 1, 1).astype(BF16)

    for window in range(count // AREA):
        cols = slice(window * AREA, (window + 1) * AREA)
        block_row, block_col, _ = window_place(
            iota((AREA, 1), 0) + window * AREA, row_shift, col_shift
        )
        kinds = jnp.zeros((AREA, 1), jnp.int32)
        for r in range(2):
            for c in range(3):
                kind = kind_ref[
                    lax.rem(lat + r, lats), lax.rem(lon * 2 + c, lons * 2)
                ]
                kinds = jnp.where((block_row == r) & (block_col == c), kind, kinds)
        for start in range(0, width, group):
            lanes = slice(start, start + group)
            bias = jnp.where(
                kinds == 0,
                kind_bias[0][:, lanes],
                jnp.where(kinds == 1, kind_bias[1][:, lanes], kind_bias[2][:, lanes]),
            )
            k, v = proj[1, cols, lanes], proj[2, cols, lanes]
            q_wide = jnp.concatenate([proj[0, cols, lanes]] * per_group, axis=0) * block_mask
            d_wide = jnp.concatenate([proj[3, cols, lanes]] * per_group, axis=0) * block_mask
            logits = dot(k, q_wide, 1, 1) * scale + bias
            logits = jnp.where(allowed, logits, -jnp.inf)
            expo = jnp.exp(logits - jnp.max(logits, axis=0, keepdims=True))
            weights = expo / jnp.sum(expo, axis=0, keepdims=True)
            d_weights = dot(v, d_wide, 1, 1)
            inner = jnp.sum(weights * d_weights, axis=0, keepdims=True)
            d_logits = (scale * weights * (d_weights - inner)).astype(BF16)
            d_proj[2, cols, lanes] = dot(weights.astype(BF16), d_wide, 1, 0).astype(BF16)
            d_proj[1, cols, lanes] = dot(d_logits, q_wide, 1, 0).astype(BF16)
            d_query_wide = dot(d_logits, k, 0, 0)
            d_query = jnp.zeros((AREA, group), F32)
            for index in range(per_group):
                d_query = jnp.where(
                    group_head == index,
                    d_query_wide[index * AREA : (index + 1) * AREA],
                    d_query,
                )
            d_proj[0, cols, lanes] = d_query.astype(BF16)

    slab = model // heads

    def partial_sum(owner):
        features = pl.ds(pl.multiple_of(owner * slab, slab), slab)
        total = dot(d_proj[0], wq[0, features], 1, 1)
        for index in range(1, 3):
            total = total + dot(d_proj[index], wq[index, features], 1, 1)
        return total

    parts = []
    for step, mate in enumerate(mates):
        part_out[step] = partial_sum(mate)
        copy = pltpu.make_async_remote_copy(
            src_ref=part_out.at[step],
            dst_ref=part_in.at[step],
            send_sem=part_send.at[step],
            recv_sem=part_recv.at[step],
            device_id={"head": mate},
            device_id_type=MESH,
        )
        copy.start()
        parts.append(copy)
    d_normed = partial_sum(head)
    for step, copy in enumerate(parts):
        copy.wait_recv()
        d_normed = d_normed + part_in[step]

    ret_out[...] = (
        dot(scatter, d_normed.astype(BF16), 1, 0).astype(BF16).reshape(6, AREA, slab)
    )

    def give_back(source, target, length, slot, device):
        copy = pltpu.make_async_remote_copy(
            src_ref=ret_out.at[pl.ds(source, length)],
            dst_ref=ret_in.at[pl.ds(target, length)],
            send_sem=ret_send.at[slot],
            recv_sem=ret_recv.at[slot],
            device_id=device,
            device_id_type=MESH,
        )
        copy.start()
        return copy

    returns = [
        give_back(5, 3, 1, 0, {"lon": right, "lat": down}),
        give_back(2, 0, 1, 1, {"lon": right}),
        give_back(3, 1, 2, 2, {"lat": down}),
    ]
    for copy in returns:
        copy.wait_recv()
    joined[head, 0:AREA] = ret_out[0] + ret_in[0] + ret_in[1] + ret_in[3]
    joined[head, AREA:] = ret_out[1] + ret_in[2]
    joins = []
    for step, mate in enumerate(mates):
        copy = pltpu.make_async_remote_copy(
            src_ref=joined.at[head],
            dst_ref=joined.at[head],
            send_sem=join_send.at[step],
            recv_sem=join_recv.at[step],
            device_id={"head": mate},
            device_id_type=MESH,
        )
        copy.start()
        joins.append(copy)
    for copy in joins:
        copy.wait_recv()
    whole = jnp.concatenate([joined[index] for index in range(heads)], axis=1)
    scaled = dot(from_blocks, whole, 1, 0) * gain
    tok = tok_ref[...].astype(F32)
    row_inner = jnp.mean(tok * scaled, axis=-1, keepdims=True)
    out_ref[...] = (
        cot_ref[...].astype(F32)
        + inverse * scaled
        - tok * (inverse * inverse * inverse) * row_inner
    ).astype(BF16)

    for copy in [from_below, from_right, from_below_next, from_corner]:
        copy.wait_send()
    for copy in forwards + parts + returns + joins:
        copy.wait_send()


def on_device(
    sizes, tokens, cotangent, w_qkv, w_out, norm_gain, type_bias, offsets, window_kind
):
    tile_rows, tile_cols, model = tokens.shape
    width = w_out.shape[0]
    heads = sizes[2]
    count = tile_rows * tile_cols
    mates = max(heads - 1, 1)
    slab = model // heads
    vmem = pl.BlockSpec(memory_space=pltpu.VMEM)
    smem = pl.BlockSpec(memory_space=pltpu.SMEM)
    hbm = pl.BlockSpec(memory_space=pl.ANY)
    result = pl.pallas_call(
        functools.partial(kernel, sizes),
        out_shape=jax.ShapeDtypeStruct((count, model), BF16),
        in_specs=[smem, smem, smem, vmem, vmem, vmem, hbm, hbm],
        out_specs=vmem,
        scratch_shapes=[
            pltpu.VMEM((6, 2, AREA, model), BF16),
            pltpu.VMEM(w_qkv.shape, BF16),
            pltpu.VMEM(w_out.shape, BF16),
            pltpu.VMEM((4, count, width), BF16),
            pltpu.VMEM((3, count, width), BF16),
            pltpu.VMEM((mates, count, slab), F32),
            pltpu.VMEM((mates, count, slab), F32),
            pltpu.VMEM((6, AREA, slab), BF16),
            pltpu.VMEM((4, AREA, slab), BF16),
            pltpu.VMEM((heads, count, slab), BF16),
            pltpu.SemaphoreType.DMA((2,)),
            pltpu.SemaphoreType.DMA((4,)),
            pltpu.SemaphoreType.DMA((4,)),
            pltpu.SemaphoreType.DMA((4, mates)),
            pltpu.SemaphoreType.DMA((4, mates)),
            pltpu.SemaphoreType.DMA((mates,)),
            pltpu.SemaphoreType.DMA((mates,)),
            pltpu.SemaphoreType.DMA((3,)),
            pltpu.SemaphoreType.DMA((3,)),
            pltpu.SemaphoreType.DMA((mates,)),
            pltpu.SemaphoreType.DMA((mates,)),
        ],
        compiler_params=pltpu.CompilerParams(
            collective_id=0, has_side_effects=True, vmem_limit_bytes=40 * 1024 * 1024
        ),
    )(
        offsets,
        window_kind,
        type_bias,
        norm_gain.reshape(1, model),
        tokens.reshape(count, model),
        cotangent.reshape(count, model),
        w_qkv,
        w_out,
    )
    return result.reshape(tokens.shape)


def solution(mesh):
    sizes = (mesh.shape["lon"], mesh.shape["lat"], mesh.shape["head"])
    return jax.shard_map(
        functools.partial(on_device, sizes),
        mesh=mesh,
        in_specs=(
            P("lat", "lon", None),
            P("lat", "lon", None),
            P(None, None, "head"),
            P("head", None),
            P(),
            P(None, "head"),
            P(),
            P(),
        ),
        out_specs=P("lat", "lon", None),
        check_vma=False,
    )
```

time: 146 us -> 40.1 us (0.27)
  the two profiles are of different devices: /device:TPU:9 before, /device:TPU:1 now
where the time goes in v1:
time: 40.1 us; the launch traced here: 39.8 us
  Pallas kernels  31.3 us (78%)
  local copies, waits for them, and re-layouts  8.42 us (21%)
    pallas_call x1, Pallas kernels, on_device(): pl.pallas_call(functools.partial(kernel, sizes), out_shape=jax.ShapeDtype...  31.3 us
    unnamed x17, local copies, waits for them, and re-layouts  8.42 us

profile of v1, /device:TPU:1, one launch (start us, length us, event | category | flops | bytes accessed | tf_op | source)
XLA Modules:
  0.0 39.8 jit_solution(7695851147842850572)
XLA Ops:
  0.0 0.0 copy-start
  0.0 1.9 %copy-done = bf16[3,1024,512]{2,1,0:T(8,128)(2,1)S(1)} copy-done((bf16[3,1024,512]{2,1,0:T(8,128)(2,1)S(1)}, bf16[3,1024,512]{2,1,0:T(8,128)(2,1)}, u32[]{:S(2)}) %copy-start) | copy-done | bytes 3145752
  1.9 0.0 copy-start.1
  1.9 1.2 %copy-done.1 = bf16[512,1024]{1,0:T(8,128)(2,1)S(1)} copy-done((bf16[512,1024]{1,0:T(8,128)(2,1)S(1)}, bf16[512,1024]{1,0:T(8,128)(2,1)}, u32[]{:S(2)}) %copy-start.1) | copy-done | bytes 1048600
  3.1 0.0 copy-start.2
  3.1 0.9 %copy-done.2 = bf16[8,16,1024]{2,1,0:T(8,128)(2,1)S(1)} copy-done((bf16[8,16,1024]{2,1,0:T(8,128)(2,1)S(1)}, bf16[8,16,1024]{2,1,0:T(8,128)(2,1)}, u32[]{:S(2)}) %copy-start.2) | copy-done | bytes 262168
  4.1 0.0 copy-start.3
  4.1 0.9 %copy-done.3 = bf16[8,16,1024]{2,1,0:T(8,128)(2,1)S(1)} copy-done((bf16[8,16,1024]{2,1,0:T(8,128)(2,1)S(1)}, bf16[8,16,1024]{2,1,0:T(8,128)(2,1)}, u32[]{:S(2)}) %copy-start.3) | copy-done | bytes 262168
  5.0 0.0 copy-start.4
  5.0 0.7 %copy-done.4 = f32[1024]{0:T(1024)S(1)} copy-done((f32[1024]{0:T(1024)S(1)}, f32[1024]{0:T(1024)}, u32[]{:S(2)}) %copy-start.4) | copy-done | bytes 4120
  5.7 0.0 copy-start.5
  5.7 0.7 %copy-done.5 = s32[4,8]{1,0:T(4,128)S(1)} copy-done((s32[4,8]{1,0:T(4,128)S(1)}, s32[4,8]{1,0:T(4,128)}, u32[]{:S(2)}) %copy-start.5) | copy-done | bytes 152
  6.4 0.0 copy-start.6
  6.4 0.7 %copy-done.6 = f32[3,8]{1,0:T(4,128)S(1)} copy-done((f32[3,8]{1,0:T(4,128)S(1)}, f32[3,8]{1,0:T(4,128)}, u32[]{:S(2)}) %copy-start.6) | copy-done | bytes 120
  7.1 0.0 copy-start.7
  7.1 0.7 %copy-done.7 = s32[2]{0:T(128)S(1)} copy-done((s32[2]{0:T(128)S(1)}, s32[2]{0:T(128)}, u32[]{:S(2)}) %copy-start.7) | copy-done | bytes 32
  7.7 31.3 %shard_map.82 = bf16[128,1024]{1,0:T(8,128)(2,1)S(1)} custom-call(s32[2]{0:T(128)S(1)} %copy-done.7, s32[4,8]{1,0:T(4,128)S(1)} %copy-done.5, f32[3,8]{1,0:T(4,128)S(1)} %copy-done.6, f32[1,1024]{1,0:T(1,128)S(1)} %bitcast.7, bf16[128,1024]{1,0:T(8,128)(2,1)S(1)} %bitcast.5, bf16[128,1024]{1,0:T(8,128)(2,1)S(1)} %bitcast.6, ...), custom_call_target="tpu_custom_call" | custom-call | tf_op jit(solution)/shard_map/pallas_call | solution.py:334
  39.0 0.7 %copy.10 = bf16[8,16,1024]{2,1,0:T(8,128)(2,1)} copy(bf16[8,16,1024]{2,1,0:T(8,128)(2,1)S(1)} %bitcast.4) | data formatting | bytes 524288
Async XLA Ops:
  0.0 1.9 %copy-start = (bf16[3,1024,512]{2,1,0:T(8,128)(2,1)S(1)}, bf16[3,1024,512]{2,1,0:T(8,128)(2,1)}, u32[]{:S(2)}) copy-start(bf16[3,1024,512]{2,1,0:T(8,128)(2,1)} %wq_hbm.1) | copy-start | bytes 9437188
  1.9 1.2 %copy-start.1 = (bf16[512,1024]{1,0:T(8,128)(2,1)S(1)}, bf16[512,1024]{1,0:T(8,128)(2,1)}, u32[]{:S(2)}) copy-start(bf16[512,1024]{1,0:T(8,128)(2,1)} %wo_hbm.1) | copy-start | bytes 3145732
  3.1 0.9 %copy-start.2 = (bf16[8,16,1024]{2,1,0:T(8,128)(2,1)S(1)}, bf16[8,16,1024]{2,1,0:T(8,128)(2,1)}, u32[]{:S(2)}) copy-start(bf16[8,16,1024]{2,1,0:T(8,128)(2,1)} %param.8) | copy-start | bytes 786436
  4.1 0.9 %copy-start.3 = (bf16[8,16,1024]{2,1,0:T(8,128)(2,1)S(1)}, bf16[8,16,1024]{2,1,0:T(8,128)(2,1)}, u32[]{:S(2)}) copy-start(bf16[8,16,1024]{2,1,0:T(8,128)(2,1)} %param.9) | copy-start | bytes 786436
  5.0 0.7 %copy-start.4 = (f32[1024]{0:T(1024)S(1)}, f32[1024]{0:T(1024)}, u32[]{:S(2)}) copy-start(f32[1024]{0:T(1024)} %param.12) | copy-start | bytes 12292
  5.7 0.7 %copy-start.5 = (s32[4,8]{1,0:T(4,128)S(1)}, s32[4,8]{1,0:T(4,128)}, u32[]{:S(2)}) copy-start(s32[4,8]{1,0:T(4,128)} %kind_ref.1) | copy-start | bytes 388
  6.4 0.7 %copy-start.6 = (f32[3,8]{1,0:T(4,128)S(1)}, f32[3,8]{1,0:T(4,128)}, u32[]{:S(2)}) copy-start(f32[3,8]{1,0:T(4,128)} %bias_ref.1) | copy-start | bytes 292
  7.1 0.7 %copy-start.7 = (s32[2]{0:T(128)S(1)}, s32[2]{0:T(128)}, u32[]{:S(2)}) copy-start(s32[2]{0:T(128)} %off_ref.1) | copy-start | bytes 28

commit v2 on v1

--- a/solution.py
+++ b/solution.py
@@ -37,15 +37,21 @@
 
 def kernel(
     sizes,
+    off_hbm,
+    kind_hbm,
+    bias_hbm,
+    gain_hbm,
+    tok_hbm,
+    cot_hbm,
+    wq_hbm,
+    wo_hbm,
+    out_ref,
     off_ref,
     kind_ref,
     bias_ref,
     gain_ref,
     tok_ref,
     cot_ref,
-    wq_hbm,
-    wo_hbm,
-    out_ref,
     cells,
     wq,
     wo,
@@ -76,10 +82,23 @@
     up, down = lax.rem(lat + lats - 1, lats), lax.rem(lat + 1, lats)
     mates = [lax.rem(head + step, heads) for step in range(1, heads)]
 
-    load_q = pltpu.make_async_copy(wq_hbm, wq, load_sem.at[0])
-    load_o = pltpu.make_async_copy(wo_hbm, wo, load_sem.at[1])
-    load_q.start()
-    load_o.start()
+    loads = [
+        pltpu.make_async_copy(source, target, load_sem.at[slot])
+        for slot, (source, target) in enumerate(
+            [
+                (tok_hbm, tok_ref),
+                (cot_hbm, cot_ref),
+                (gain_hbm, gain_ref),
+                (off_hbm, off_ref),
+                (kind_hbm, kind_ref),
+                (bias_hbm, bias_ref),
+                (wq_hbm, wq),
+                (wo_hbm, wo),
+            ]
+        )
+    ]
+    for load in loads:
+        load.start()
 
     barrier = pltpu.get_barrier_semaphore()
     partners = [
@@ -87,64 +106,69 @@
         {"lon": right},
         {"lat": up},
         {"lat": down},
-        {"lon": right, "lat": down},
-        {"lon": left, "lat": up},
     ] + [{"head": mate} for mate in mates]
     for partner in partners:
         pl.semaphore_signal(barrier, inc=1, device_id=partner, device_id_type=MESH)
 
+    big, small = iota((count, count), 0), iota((count, count), 1)
+
+    def natural(flat):
+        return (((flat >> 3) & 7) << 4) + ((flat >> 6) << 3) + (flat & 7)
+
+    to_blocks = one_hot(natural(big) == small)
+    from_blocks = one_hot(natural(small) == big)
+    loads[1].wait()
+    cells[0:2, 0] = dot(to_blocks, cot_ref[...], 1, 0).astype(BF16).reshape(2, AREA, model)
+
+    pl.semaphore_wait(barrier, len(partners))
+
+    share = AREA // heads
+    rows = pl.ds(pl.multiple_of(head * share, share), share)
+
+    def near(source, target, array, slot, device):
+        return pltpu.make_async_remote_copy(
+            src_ref=cells.at[source, array, rows],
+            dst_ref=cells.at[target, array, rows],
+            send_sem=near_send.at[slot, array],
+            recv_sem=near_recv.at[slot, array],
+            device_id=device,
+            device_id_type=MESH,
+        )
+
+    from_below = [near(0, 3, array, 0, {"lat": up}) for array in range(2)]
+    from_right = [near(0, 2, array, 1, {"lon": left}) for array in range(2)]
+    from_below_next = [near(1, 4, array, 2, {"lat": up}) for array in range(2)]
+    from_corner = [near(3, 5, array, 3, {"lon": left}) for array in range(2)]
+    from_below[0].start()
+    from_right[0].start()
+
+    loads[0].wait()
+    loads[2].wait()
     gain = gain_ref[...]
     tok = tok_ref[...].astype(F32)
     inverse = lax.rsqrt(jnp.mean(tok * tok, axis=-1, keepdims=True) + EPSILON)
     normed = (tok * inverse * gain).astype(BF16)
-    big, small = iota((count, count), 0), iota((count, count), 1)
-
-    def natural(flat):
-        return (((flat >> 3) & 7) << 4) + ((flat >> 6) << 3) + (flat & 7)
-
-    to_blocks = one_hot(natural(big) == small)
-    from_blocks = one_hot(natural(small) == big)
-    cells[0:2, 0] = dot(to_blocks, normed, 1, 0).astype(BF16).reshape(2, AREA, model)
-    cells[0:2, 1] = dot(to_blocks, cot_ref[...], 1, 0).astype(BF16).reshape(2, AREA, model)
-
-    pl.semaphore_wait(barrier, len(partners))
-
-    share = AREA // heads
-    rows = pl.ds(pl.multiple_of(head * share, share), share)
-
-    def near(source, target, slot, device):
-        return pltpu.make_async_remote_copy(
-            src_ref=cells.at[source, :, rows],
-            dst_ref=cells.at[target, :, rows],
-            send_sem=near_send.at[slot],
-            recv_sem=near_recv.at[slot],
-            device_id=device,
-            device_id_type=MESH,
-        )
-
-    from_below = near(0, 3, 0, {"lat": up})
-    from_right = near(0, 2, 1, {"lon": left})
-    from_below_next = near(1, 4, 2, {"lat": up})
-    from_corner = near(3, 5, 3, {"lon": left})
-    from_below.start()
-    from_right.start()
-    from_below_next.start()
+    cells[0:2, 1] = dot(to_blocks, normed, 1, 0).astype(BF16).reshape(2, AREA, model)
+    from_below[1].start()
+    from_right[1].start()
 
     forwards = []
 
-    def forward(block, slot):
+    def forward(block, array, slot):
         for step, mate in enumerate(mates):
             copy = pltpu.make_async_remote_copy(
-                src_ref=cells.at[block, :, rows],
-                dst_ref=cells.at[block, :, rows],
-                send_sem=fwd_send.at[slot, step],
-                recv_sem=fwd_recv.at[slot, step],
+                src_ref=cells.at[block, array, rows],
+                dst_ref=cells.at[block, array, rows],
+                send_sem=fwd_send.at[slot, array, step],
+                recv_sem=fwd_recv.at[slot, array, step],
                 device_id={"head": mate},
                 device_id_type=MESH,
             )
             copy.start()
             forwards.append(copy)
 
+    for load in loads[3:6]:
+        load.wait()
     row_shift, col_shift = off_ref[0], off_ref[1]
     place_r = window_place(iota((count, 6 * AREA), 0), row_shift, col_shift)
     gather = one_hot(
@@ -176,22 +200,29 @@
     edge = lats * WIN - lat * WIN - row_shift
     allowed = (key_row >= edge) == (query_row >= edge)
 
-    from_right.wait_recv()
-    forward(2, 1)
-    from_below.wait_recv()
-    from_corner.start()
-    forward(3, 0)
-    from_below_next.wait_recv()
-    forward(4, 2)
-    load_q.wait()
-    load_o.wait()
-    from_corner.wait_recv()
-    forward(5, 3)
+    for array in range(2):
+        from_below[array].wait_send()
+        from_below_next[array].start()
+    for array in range(2):
+        from_below[array].wait_recv()
+        from_corner[array].start()
+        forward(3, array, 0)
+    for array in range(2):
+        from_right[array].wait_recv()
+        forward(2, array, 1)
+    for array in range(2):
+        from_below_next[array].wait_recv()
+        forward(4, array, 2)
+    loads[6].wait()
+    loads[7].wait()
+    for array in range(2):
+        from_corner[array].wait_recv()
+        forward(5, array, 3)
     for copy in forwards:
         copy.wait_recv()
 
-    picked = dot(gather, cells[:, 0].reshape(6 * AREA, model), 1, 0).astype(BF16)
-    picked_cot = dot(gather, cells[:, 1].reshape(6 * AREA, model), 1, 0).astype(BF16)
+    picked = dot(gather, cells[:, 1].reshape(6 * AREA, model), 1, 0).astype(BF16)
+    picked_cot = dot(gather, cells[:, 0].reshape(6 * AREA, model), 1, 0).astype(BF16)
     for index in range(3):
         proj[index] = dot(picked, wq[index], 1, 0).astype(BF16)
     proj[3] = dot(picked_cot, wo[...], 1, 1).astype(BF16)
@@ -268,10 +299,10 @@
         dot(scatter, d_normed.astype(BF16), 1, 0).astype(BF16).reshape(6, AREA, slab)
     )
 
-    def give_back(source, target, length, slot, device):
+    def give_back(source, slot, device):
         copy = pltpu.make_async_remote_copy(
-            src_ref=ret_out.at[pl.ds(source, length)],
-            dst_ref=ret_in.at[pl.ds(target, length)],
+            src_ref=ret_out.at[source],
+            dst_ref=ret_in.at[slot],
             send_sem=ret_send.at[slot],
             recv_sem=ret_recv.at[slot],
             device_id=device,
@@ -280,15 +311,18 @@
         copy.start()
         return copy
 
-    returns = [
-        give_back(5, 3, 1, 0, {"lon": right, "lat": down}),
-        give_back(2, 0, 1, 1, {"lon": right}),
-        give_back(3, 1, 2, 2, {"lat": down}),
-    ]
-    for copy in returns:
-        copy.wait_recv()
-    joined[head, 0:AREA] = ret_out[0] + ret_in[0] + ret_in[1] + ret_in[3]
-    joined[head, AREA:] = ret_out[1] + ret_in[2]
+    corner = give_back(5, 0, {"lon": right})
+    next_down = give_back(4, 1, {"lat": down})
+    aside = give_back(2, 2, {"lon": right})
+    corner.wait_recv()
+    ret_out[3] = ret_out[3] + ret_in[0]
+    first_down = give_back(3, 3, {"lat": down})
+    next_down.wait_recv()
+    joined[head, AREA:] = ret_out[1] + ret_in[1]
+    aside.wait_recv()
+    first_down.wait_recv()
+    joined[head, 0:AREA] = ret_out[0] + ret_in[2] + ret_in[3]
+    returns = [corner, next_down, aside, first_down]
     joins = []
     for step, mate in enumerate(mates):
         copy = pltpu.make_async_remote_copy(
@@ -313,7 +347,7 @@
         - tok * (inverse * inverse * inverse) * row_inner
     ).astype(BF16)
 
-    for copy in [from_below, from_right, from_below_next, from_corner]:
+    for copy in from_right + from_below_next + from_corner:
         copy.wait_send()
     for copy in forwards + parts + returns + joins:
         copy.wait_send()
@@ -329,14 +363,19 @@
     mates = max(heads - 1, 1)
     slab = model // heads
     vmem = pl.BlockSpec(memory_space=pltpu.VMEM)
-    smem = pl.BlockSpec(memory_space=pltpu.SMEM)
     hbm = pl.BlockSpec(memory_space=pl.ANY)
     result = pl.pallas_call(
         functools.partial(kernel, sizes),
         out_shape=jax.ShapeDtypeStruct((count, model), BF16),
-        in_specs=[smem, smem, smem, vmem, vmem, vmem, hbm, hbm],
+        in_specs=[hbm] * 8,
         out_specs=vmem,
         scratch_shapes=[
+            pltpu.SMEM(offsets.shape, jnp.int32),
+            pltpu.SMEM(window_kind.shape, jnp.int32),
+            pltpu.SMEM(type_bias.shape, F32),
+            pltpu.VMEM((1, model), F32),
+            pltpu.VMEM((count, model), BF16),
+            pltpu.VMEM((count, model), BF16),
             pltpu.VMEM((6, 2, AREA, model), BF16),
             pltpu.VMEM(w_qkv.shape, BF16),
             pltpu.VMEM(w_out.shape, BF16),
@@ -347,20 +386,20 @@
             pltpu.VMEM((6, AREA, slab), BF16),
             pltpu.VMEM((4, AREA, slab), BF16),
             pltpu.VMEM((heads, count, slab), BF16),
-            pltpu.SemaphoreType.DMA((2,)),
+            pltpu.SemaphoreType.DMA((8,)),
+            pltpu.SemaphoreType.DMA((4, 2)),
+            pltpu.SemaphoreType.DMA((4, 2)),
+            pltpu.SemaphoreType.DMA((4, 2, mates)),
+            pltpu.SemaphoreType.DMA((4, 2, mates)),
+            pltpu.SemaphoreType.DMA((mates,)),
+            pltpu.SemaphoreType.DMA((mates,)),
             pltpu.SemaphoreType.DMA((4,)),
             pltpu.SemaphoreType.DMA((4,)),
-            pltpu.SemaphoreType.DMA((4, mates)),
-            pltpu.SemaphoreType.DMA((4, mates)),
-            pltpu.SemaphoreType.DMA((mates,)),
-            pltpu.SemaphoreType.DMA((mates,)),
-            pltpu.SemaphoreType.DMA((3,)),
-            pltpu.SemaphoreType.DMA((3,)),
             pltpu.SemaphoreType.DMA((mates,)),
             pltpu.SemaphoreType.DMA((mates,)),
         ],
         compiler_params=pltpu.CompilerParams(
-            collective_id=0, has_side_effects=True, vmem_limit_bytes=40 * 1024 * 1024
+            collective_id=0, has_side_effects=True, vmem_limit_bytes=63 * 1024 * 1024
         ),
     )(
         offsets,

time: 40.1 us -> 32.9 us (0.82)
  local copies, waits for them, and re-layouts: 8.42 us -> 1.67 us
    unnamed x17 -> x1, local copies, waits for them, and re-layouts: 8.42 us -> 1.67 us
where the time goes in v2:
time: 32.9 us; the launch traced here: 32.7 us
  Pallas kernels  31.1 us (95%)
  local copies, waits for them, and re-layouts  1.67 us (5%)
    pallas_call x1, Pallas kernels, on_device(): pl.pallas_call(functools.partial(kernel, sizes), out_shape=jax.ShapeDtype...  31.1 us
    unnamed x1, local copies, waits for them, and re-layouts  1.67 us

profile of v2, /device:TPU:1, one launch (start us, length us, event | category | flops | bytes accessed | tf_op | source)
XLA Modules:
  0.0 32.7 jit_solution(10477917335983535168)
XLA Ops:
  0.0 31.1 %shard_map.82 = bf16[128,1024]{1,0:T(8,128)(2,1)} custom-call(s32[2]{0:T(128)} %off_hbm.1, s32[4,8]{1,0:T(4,128)} %kind_hbm.1, f32[3,8]{1,0:T(4,128)} %bias_hbm.1, f32[1,1024]{1,0:T(1,128)} %bitcast.7, bf16[128,1024]{1,0:T(8,128)(2,1)} %bitcast.5, bf16[128,1024]{1,0:T(8,128)(2,1)} %bitcast.6, bf16[3,1024,512]{2,1,0:T(8,128)(2,1)} %wq_hbm.1, ...), custom_call_target="tpu_custom_call" | custom-call | tf_op jit(solution)/shard_map/pallas_call | solution.py:367
  31.1 1.7 %copy.10 = bf16[8,16,1024]{2,1,0:T(8,128)(2,1)} copy(bf16[8,16,1024]{2,1,0:T(8,128)(2,1)} %bitcast.4) | data formatting | bytes 524288

commit v3 on v2

--- a/solution.py
+++ b/solution.py
@@ -59,6 +59,7 @@
     d_proj,
     part_out,
     part_in,
+    extra,
     ret_out,
     ret_in,
     joined,
@@ -101,14 +102,15 @@
         load.start()
 
     barrier = pltpu.get_barrier_semaphore()
-    partners = [
-        {"lon": left},
-        {"lon": right},
-        {"lat": up},
-        {"lat": down},
-    ] + [{"head": mate} for mate in mates]
-    for partner in partners:
+    has_up, has_down = lat > 0, lat < lats - 1
+
+    def greet(partner):
         pl.semaphore_signal(barrier, inc=1, device_id=partner, device_id_type=MESH)
+
+    for partner in [{"lon": left}, {"lon": right}] + [{"head": mate} for mate in mates]:
+        greet(partner)
+    pl.when(has_up)(lambda: greet({"lat": up}))
+    pl.when(has_down)(lambda: greet({"lat": down}))
 
     big, small = iota((count, count), 0), iota((count, count), 1)
 
@@ -120,7 +122,9 @@
     loads[1].wait()
     cells[0:2, 0] = dot(to_blocks, cot_ref[...], 1, 0).astype(BF16).reshape(2, AREA, model)
 
-    pl.semaphore_wait(barrier, len(partners))
+    pl.semaphore_wait(
+        barrier, 1 + heads + has_up.astype(jnp.int32) + has_down.astype(jnp.int32)
+    )
 
     share = AREA // heads
     rows = pl.ds(pl.multiple_of(head * share, share), share)
@@ -139,7 +143,7 @@
     from_right = [near(0, 2, array, 1, {"lon": left}) for array in range(2)]
     from_below_next = [near(1, 4, array, 2, {"lat": up}) for array in range(2)]
     from_corner = [near(3, 5, array, 3, {"lon": left}) for array in range(2)]
-    from_below[0].start()
+    pl.when(has_up)(from_below[0].start)
     from_right[0].start()
 
     loads[0].wait()
@@ -149,14 +153,12 @@
     inverse = lax.rsqrt(jnp.mean(tok * tok, axis=-1, keepdims=True) + EPSILON)
     normed = (tok * inverse * gain).astype(BF16)
     cells[0:2, 1] = dot(to_blocks, normed, 1, 0).astype(BF16).reshape(2, AREA, model)
-    from_below[1].start()
+    pl.when(has_up)(from_below[1].start)
     from_right[1].start()
 
-    forwards = []
-
-    def forward(block, array, slot):
-        for step, mate in enumerate(mates):
-            copy = pltpu.make_async_remote_copy(
+    def forwards(block, array, slot):
+        return [
+            pltpu.make_async_remote_copy(
                 src_ref=cells.at[block, array, rows],
                 dst_ref=cells.at[block, array, rows],
                 send_sem=fwd_send.at[slot, array, step],
@@ -164,21 +166,16 @@
                 device_id={"head": mate},
                 device_id_type=MESH,
             )
+            for step, mate in enumerate(mates)
+        ]
+
+    def forward(block, array, slot):
+        for copy in forwards(block, array, slot):
             copy.start()
-            forwards.append(copy)
 
     for load in loads[3:6]:
         load.wait()
     row_shift, col_shift = off_ref[0], off_ref[1]
-    place_r = window_place(iota((count, 6 * AREA), 0), row_shift, col_shift)
-    gather = one_hot(
-        ((place_r[0] * 3 + place_r[1]) << 6) + place_r[2] == iota((count, 6 * AREA), 1)
-    )
-    place_c = window_place(iota((6 * AREA, count), 1), row_shift, col_shift)
-    scatter = one_hot(
-        ((place_c[0] * 3 + place_c[1]) << 6) + place_c[2] == iota((6 * AREA, count), 0)
-    )
-
     local_heads = bias_ref.shape[1]
     head_dim = width // local_heads
     scale = head_dim ** (-0.5)
@@ -197,77 +194,6 @@
     group_head = iota((1, group), 1) // head_dim
     query_row = (iota((AREA, group), 1) >> 3) & 7
     key_row = iota((AREA, group), 0) >> 3
-    edge = lats * WIN - lat * WIN - row_shift
-    allowed = (key_row >= edge) == (query_row >= edge)
-
-    for array in range(2):
-        from_below[array].wait_send()
-        from_below_next[array].start()
-    for array in range(2):
-        from_below[array].wait_recv()
-        from_corner[array].start()
-        forward(3, array, 0)
-    for array in range(2):
-        from_right[array].wait_recv()
-        forward(2, array, 1)
-    for array in range(2):
-        from_below_next[array].wait_recv()
-        forward(4, array, 2)
-    loads[6].wait()
-    loads[7].wait()
-    for array in range(2):
-        from_corner[array].wait_recv()
-        forward(5, array, 3)
-    for copy in forwards:
-        copy.wait_recv()
-
-    picked = dot(gather, cells[:, 1].reshape(6 * AREA, model), 1, 0).astype(BF16)
-    picked_cot = dot(gather, cells[:, 0].reshape(6 * AREA, model), 1, 0).astype(BF16)
-    for index in range(3):
-        proj[index] = dot(picked, wq[index], 1, 0).astype(BF16)
-    proj[3] = dot(picked_cot, wo[...], 1, 1).astype(BF16)
-
-    for window in range(count // AREA):
-        cols = slice(window * AREA, (window + 1) * AREA)
-        block_row, block_col, _ = window_place(
-            iota((AREA, 1), 0) + window * AREA, row_shift, col_shift
-        )
-        kinds = jnp.zeros((AREA, 1), jnp.int32)
-        for r in range(2):
-            for c in range(3):
-                kind = kind_ref[
-                    lax.rem(lat + r, lats), lax.rem(lon * 2 + c, lons * 2)
-                ]
-                kinds = jnp.where((block_row == r) & (block_col == c), kind, kinds)
-        for start in range(0, width, group):
-            lanes = slice(start, start + group)
-            bias = jnp.where(
-                kinds == 0,
-                kind_bias[0][:, lanes],
-                jnp.where(kinds == 1, kind_bias[1][:, lanes], kind_bias[2][:, lanes]),
-            )
-            k, v = proj[1, cols, lanes], proj[2, cols, lanes]
-            q_wide = jnp.concatenate([proj[0, cols, lanes]] * per_group, axis=0) * block_mask
-            d_wide = jnp.concatenate([proj[3, cols, lanes]] * per_group, axis=0) * block_mask
-            logits = dot(k, q_wide, 1, 1) * scale + bias
-            logits = jnp.where(allowed, logits, -jnp.inf)
-            expo = jnp.exp(logits - jnp.max(logits, axis=0, keepdims=True))
-            weights = expo / jnp.sum(expo, axis=0, keepdims=True)
-            d_weights = dot(v, d_wide, 1, 1)
-            inner = jnp.sum(weights * d_weights, axis=0, keepdims=True)
-            d_logits = (scale * weights * (d_weights - inner)).astype(BF16)
-            d_proj[2, cols, lanes] = dot(weights.astype(BF16), d_wide, 1, 0).astype(BF16)
-            d_proj[1, cols, lanes] = dot(d_logits, q_wide, 1, 0).astype(BF16)
-            d_query_wide = dot(d_logits, k, 0, 0)
-            d_query = jnp.zeros((AREA, group), F32)
-            for index in range(per_group):
-                d_query = jnp.where(
-                    group_head == index,
-                    d_query_wide[index * AREA : (index + 1) * AREA],
-                    d_query,
-                )
-            d_proj[0, cols, lanes] = d_query.astype(BF16)
-
     slab = model // heads
 
     def partial_sum(owner):
@@ -277,30 +203,88 @@
             total = total + dot(d_proj[index], wq[index, features], 1, 1)
         return total
 
-    parts = []
-    for step, mate in enumerate(mates):
-        part_out[step] = partial_sum(mate)
-        copy = pltpu.make_async_remote_copy(
-            src_ref=part_out.at[step],
-            dst_ref=part_in.at[step],
-            send_sem=part_send.at[step],
-            recv_sem=part_recv.at[step],
-            device_id={"head": mate},
-            device_id_type=MESH,
-        )
-        copy.start()
-        parts.append(copy)
-    d_normed = partial_sum(head)
-    for step, copy in enumerate(parts):
-        copy.wait_recv()
-        d_normed = d_normed + part_in[step]
-
-    ret_out[...] = (
-        dot(scatter, d_normed.astype(BF16), 1, 0).astype(BF16).reshape(6, AREA, slab)
-    )
+    def part_copies(turn):
+        return [
+            pltpu.make_async_remote_copy(
+                src_ref=part_out.at[turn, step],
+                dst_ref=part_in.at[turn, step],
+                send_sem=part_send.at[turn, step],
+                recv_sem=part_recv.at[turn, step],
+                device_id={"head": mate},
+                device_id_type=MESH,
+            )
+            for step, mate in enumerate(mates)
+        ]
+
+    def backward(turn, blocks, row_shift, edge):
+        span = blocks * AREA
+        place = window_place(iota((count, span), 0), row_shift, col_shift)
+        gather = one_hot(((place[0] * 3 + place[1]) << 6) + place[2] == iota((count, span), 1))
+        gather = gather * one_hot(place[0] >= 0)
+        place = window_place(iota((span, count), 1), row_shift, col_shift)
+        scatter = one_hot(((place[0] * 3 + place[1]) << 6) + place[2] == iota((span, count), 0))
+        scatter = scatter * one_hot(place[0] >= 0)
+        allowed = (key_row >= edge) == (query_row >= edge)
+        picked = dot(gather, cells[0:blocks, 1].reshape(span, model), 1, 0).astype(BF16)
+        picked_cot = dot(gather, cells[0:blocks, 0].reshape(span, model), 1, 0).astype(BF16)
+        for index in range(3):
+            proj[index] = dot(picked, wq[index], 1, 0).astype(BF16)
+        proj[3] = dot(picked_cot, wo[...], 1, 1).astype(BF16)
+
+        for window in range(count // AREA):
+            cols = slice(window * AREA, (window + 1) * AREA)
+            block_row, block_col, _ = window_place(
+                iota((AREA, 1), 0) + window * AREA, row_shift, col_shift
+            )
+            kinds = jnp.zeros((AREA, 1), jnp.int32)
+            for r in range(2):
+                for c in range(3):
+                    kind = kind_ref[
+                        lax.rem(lat + r, lats), lax.rem(lon * 2 + c, lons * 2)
+                    ]
+                    kinds = jnp.where((block_row == r) & (block_col == c), kind, kinds)
+            for start in range(0, width, group):
+                lanes = slice(start, start + group)
+                bias = jnp.where(
+                    kinds == 0,
+                    kind_bias[0][:, lanes],
+                    jnp.where(kinds == 1, kind_bias[1][:, lanes], kind_bias[2][:, lanes]),
+                )
+                k, v = proj[1, cols, lanes], proj[2, cols, lanes]
+                q_wide = jnp.concatenate([proj[0, cols, lanes]] * per_group, axis=0) * block_mask
+                d_wide = jnp.concatenate([proj[3, cols, lanes]] * per_group, axis=0) * block_mask
+                logits = dot(k, q_wide, 1, 1) * scale + bias
+                logits = jnp.where(allowed, logits, -jnp.inf)
+                expo = jnp.exp(logits - jnp.max(logits, axis=0, keepdims=True))
+                weights = expo / jnp.sum(expo, axis=0, keepdims=True)
+                d_weights = dot(v, d_wide, 1, 1)
+                inner = jnp.sum(weights * d_weights, axis=0, keepdims=True)
+                d_logits = (scale * weights * (d_weights - inner)).astype(BF16)
+                d_proj[2, cols, lanes] = dot(weights.astype(BF16), d_wide, 1, 0).astype(BF16)
+                d_proj[1, cols, lanes] = dot(d_logits, q_wide, 1, 0).astype(BF16)
+                d_query_wide = dot(d_logits, k, 0, 0)
+                d_query = jnp.zeros((AREA, group), F32)
+                for index in range(per_group):
+                    d_query = jnp.where(
+                        group_head == index,
+                        d_query_wide[index * AREA : (index + 1) * AREA],
+                        d_query,
+                    )
+                d_proj[0, cols, lanes] = d_query.astype(BF16)
+
+        copies = part_copies(turn)
+        for step, mate in enumerate(mates):
+            part_out[turn, step] = partial_sum(mate)
+            copies[step].start()
+        d_normed = partial_sum(head)
+        for step, copy in enumerate(copies):
+            copy.wait_recv()
+            d_normed = d_normed + part_in[turn, step]
+        spread = dot(scatter, d_normed.astype(BF16), 1, 0).astype(BF16)
+        return spread.reshape(blocks, AREA, slab)
 
     def give_back(source, slot, device):
-        copy = pltpu.make_async_remote_copy(
+        return pltpu.make_async_remote_copy(
             src_ref=ret_out.at[source],
             dst_ref=ret_in.at[slot],
             send_sem=ret_send.at[slot],
@@ -308,21 +292,85 @@
             device_id=device,
             device_id_type=MESH,
         )
-        copy.start()
-        return copy
+
+    @pl.when(has_up)
+    def _():
+        for array in range(2):
+            from_below[array].wait_send()
+            from_below_next[array].start()
+
+    @pl.when(has_down)
+    def _():
+        for array in range(2):
+            from_below[array].wait_recv()
+            from_corner[array].start()
+            forward(3, array, 0)
+
+    for array in range(2):
+        from_right[array].wait_recv()
+        forward(2, array, 1)
+    loads[6].wait()
+    loads[7].wait()
+    for array in range(2):
+        for copy in forwards(2, array, 1):
+            copy.wait_recv()
+
+    @pl.when(jnp.logical_not(has_up))
+    def _():
+        extra[...] = backward(1, 3, row_shift - WIN, WIN - row_shift)
+
+    @pl.when(has_down)
+    def _():
+        for array in range(2):
+            from_below_next[array].wait_recv()
+            forward(4, array, 2)
+        for array in range(2):
+            from_corner[array].wait_recv()
+            forward(5, array, 3)
+        for block, slot in [(3, 0), (4, 2), (5, 3)]:
+            for array in range(2):
+                for copy in forwards(block, array, slot):
+                    copy.wait_recv()
+
+    @pl.when(jnp.logical_not(has_down))
+    def _():
+        cells[3:6] = jnp.zeros((3, 2, AREA, model), BF16)
+
+    ret_out[...] = backward(0, 6, row_shift, lats * WIN - lat * WIN - row_shift)
+
+    @pl.when(jnp.logical_not(has_up))
+    def _():
+        ret_out[0:3] = ret_out[0:3] + extra[...]
 
     corner = give_back(5, 0, {"lon": right})
     next_down = give_back(4, 1, {"lat": down})
     aside = give_back(2, 2, {"lon": right})
-    corner.wait_recv()
-    ret_out[3] = ret_out[3] + ret_in[0]
     first_down = give_back(3, 3, {"lat": down})
-    next_down.wait_recv()
-    joined[head, AREA:] = ret_out[1] + ret_in[1]
+
+    @pl.when(has_down)
+    def _():
+        corner.start()
+        next_down.start()
+
+    aside.start()
+
+    @pl.when(has_down)
+    def _():
+        corner.wait_recv()
+        ret_out[3] = ret_out[3] + ret_in[0]
+        first_down.start()
+
     aside.wait_recv()
-    first_down.wait_recv()
-    joined[head, 0:AREA] = ret_out[0] + ret_in[2] + ret_in[3]
-    returns = [corner, next_down, aside, first_down]
+    joined[head, 0:AREA] = ret_out[0] + ret_in[2]
+    joined[head, AREA:] = ret_out[1]
+
+    @pl.when(has_up)
+    def _():
+        next_down.wait_recv()
+        joined[head, AREA:] = joined[head, AREA:] + ret_in[1]
+        first_down.wait_recv()
+        joined[head, 0:AREA] = joined[head, 0:AREA] + ret_in[3]
+
     joins = []
     for step, mate in enumerate(mates):
         copy = pltpu.make_async_remote_copy(
@@ -347,9 +395,29 @@
         - tok * (inverse * inverse * inverse) * row_inner
     ).astype(BF16)
 
-    for copy in from_right + from_below_next + from_corner:
-        copy.wait_send()
-    for copy in forwards + parts + returns + joins:
+    @pl.when(has_up)
+    def _():
+        for copy in from_below_next:
+            copy.wait_send()
+
+    @pl.when(has_down)
+    def _():
+        for copy in from_corner + [corner, next_down, first_down]:
+            copy.wait_send()
+        for block, slot in [(3, 0), (4, 2), (5, 3)]:
+            for array in range(2):
+                for copy in forwards(block, array, slot):
+                    copy.wait_send()
+
+    @pl.when(jnp.logical_not(has_up))
+    def _():
+        for copy in part_copies(1):
+            copy.wait_send()
+
+    for array in range(2):
+        for copy in forwards(2, array, 1):
+            copy.wait_send()
+    for copy in from_right + part_copies(0) + [aside] + joins:
         copy.wait_send()
 
 
@@ -381,8 +449,9 @@
             pltpu.VMEM(w_out.shape, BF16),
             pltpu.VMEM((4, count, width), BF16),
             pltpu.VMEM((3, count, width), BF16),
-            pltpu.VMEM((mates, count, slab), F32),
-            pltpu.VMEM((mates, count, slab), F32),
+            pltpu.VMEM((2, mates, count, slab), F32),
+            pltpu.VMEM((2, mates, count, slab), F32),
+            pltpu.VMEM((3, AREA, slab), BF16),
             pltpu.VMEM((6, AREA, slab), BF16),
             pltpu.VMEM((4, AREA, slab), BF16),
             pltpu.VMEM((heads, count, slab), BF16),
@@ -391,8 +460,8 @@
             pltpu.SemaphoreType.DMA((4, 2)),
             pltpu.SemaphoreType.DMA((4, 2, mates)),
             pltpu.SemaphoreType.DMA((4, 2, mates)),
-            pltpu.SemaphoreType.DMA((mates,)),
-            pltpu.SemaphoreType.DMA((mates,)),
+            pltpu.SemaphoreType.DMA((2, mates)),
+            pltpu.SemaphoreType.DMA((2, mates)),
             pltpu.SemaphoreType.DMA((4,)),
             pltpu.SemaphoreType.DMA((4,)),
             pltpu.SemaphoreType.DMA((mates,)),

time: 32.9 us -> 31.2 us (0.948)
  the two profiles are of different devices: /device:TPU:1 before, /device:TPU:9 now
where the time goes in v3:
time: 31.2 us; the launch traced here: 31.1 us
  Pallas kernels  29.4 us (94%)
  local copies, waits for them, and re-layouts  1.67 us (5%)
    pallas_call x1, Pallas kernels, on_device(): pl.pallas_call(functools.partial(kernel, sizes), out_shape=jax.ShapeDtype...  29.4 us
    unnamed x1, local copies, waits for them, and re-layouts  1.67 us

profile of v3, /device:TPU:9, one launch (start us, length us, event | category | flops | bytes accessed | tf_op | source)
XLA Modules:
  0.0 31.1 jit_solution(9704304179814245831)
XLA Ops:
  0.0 29.4 %shard_map.82 = bf16[128,1024]{1,0:T(8,128)(2,1)} custom-call(s32[2]{0:T(128)} %off_hbm.1, s32[4,8]{1,0:T(4,128)} %kind_hbm.1, f32[3,8]{1,0:T(4,128)} %bias_hbm.1, f32[1,1024]{1,0:T(1,128)} %bitcast.7, bf16[128,1024]{1,0:T(8,128)(2,1)} %bitcast.5, bf16[128,1024]{1,0:T(8,128)(2,1)} %bitcast.6, bf16[3,1024,512]{2,1,0:T(8,128)(2,1)} %wq_hbm.1, ...), custom_call_target="tpu_custom_call" | custom-call | tf_op jit(solution)/shard_map/pallas_call | solution.py:435
  29.4 1.7 %copy.10 = bf16[8,16,1024]{2,1,0:T(8,128)(2,1)} copy(bf16[8,16,1024]{2,1,0:T(8,128)(2,1)} %bitcast.4) | data formatting | bytes 524288

commit v4 on v3

--- a/solution.py
+++ b/solution.py
@@ -59,6 +59,8 @@
     d_proj,
     part_out,
     part_in,
+    part_own,
+    chosen,
     extra,
     ret_out,
     ret_in,
@@ -216,17 +218,15 @@
             for step, mate in enumerate(mates)
         ]
 
-    def backward(turn, blocks, row_shift, edge):
-        span = blocks * AREA
-        place = window_place(iota((count, span), 0), row_shift, col_shift)
-        gather = one_hot(((place[0] * 3 + place[1]) << 6) + place[2] == iota((count, span), 1))
-        gather = gather * one_hot(place[0] >= 0)
-        place = window_place(iota((span, count), 1), row_shift, col_shift)
-        scatter = one_hot(((place[0] * 3 + place[1]) << 6) + place[2] == iota((span, count), 0))
-        scatter = scatter * one_hot(place[0] >= 0)
+    def gather(first, last, row_shift, array):
+        span = (last - first) * AREA
+        block_row, block_col, inside = window_place(iota((count, span), 0), row_shift, col_shift)
+        source = ((block_row * 3 + block_col) << 6) + inside
+        picks = one_hot(source == iota((count, span), 1) + first * AREA)
+        return dot(picks, cells[first:last, array].reshape(span, model), 1, 0).astype(BF16)
+
+    def begin(turn, picked, picked_cot, row_shift, edge):
         allowed = (key_row >= edge) == (query_row >= edge)
-        picked = dot(gather, cells[0:blocks, 1].reshape(span, model), 1, 0).astype(BF16)
-        picked_cot = dot(gather, cells[0:blocks, 0].reshape(span, model), 1, 0).astype(BF16)
         for index in range(3):
             proj[index] = dot(picked, wq[index], 1, 0).astype(BF16)
         proj[3] = dot(picked_cot, wo[...], 1, 1).astype(BF16)
@@ -276,8 +276,15 @@
         for step, mate in enumerate(mates):
             part_out[turn, step] = partial_sum(mate)
             copies[step].start()
-        d_normed = partial_sum(head)
-        for step, copy in enumerate(copies):
+        part_own[turn] = partial_sum(head)
+
+    def finish(turn, blocks, row_shift):
+        span = blocks * AREA
+        block_row, block_col, inside = window_place(iota((span, count), 1), row_shift, col_shift)
+        target = ((block_row * 3 + block_col) << 6) + inside
+        scatter = one_hot(target == iota((span, count), 0))
+        d_normed = part_own[turn]
+        for step, copy in enumerate(part_copies(turn)):
             copy.wait_recv()
             d_normed = d_normed + part_in[turn, step]
         spread = dot(scatter, d_normed.astype(BF16), 1, 0).astype(BF16)
@@ -317,7 +324,21 @@
 
     @pl.when(jnp.logical_not(has_up))
     def _():
-        extra[...] = backward(1, 3, row_shift - WIN, WIN - row_shift)
+        shift = row_shift - WIN
+        begin(1, gather(0, 3, shift, 1), gather(0, 3, shift, 0), shift, WIN - row_shift)
+
+    @pl.when(jnp.logical_not(has_down))
+    def _():
+        cells[3:6] = jnp.zeros((3, 2, AREA, model), BF16)
+
+    @pl.when(has_down)
+    def _():
+        for array in range(2):
+            for copy in forwards(3, array, 0):
+                copy.wait_recv()
+
+    for array in range(2):
+        chosen[array] = gather(0, 4, row_shift, array)
 
     @pl.when(has_down)
     def _():
@@ -327,16 +348,24 @@
         for array in range(2):
             from_corner[array].wait_recv()
             forward(5, array, 3)
-        for block, slot in [(3, 0), (4, 2), (5, 3)]:
+        for block, slot in [(4, 2), (5, 3)]:
             for array in range(2):
                 for copy in forwards(block, array, slot):
                     copy.wait_recv()
 
-    @pl.when(jnp.logical_not(has_down))
-    def _():
-        cells[3:6] = jnp.zeros((3, 2, AREA, model), BF16)
-
-    ret_out[...] = backward(0, 6, row_shift, lats * WIN - lat * WIN - row_shift)
+    begin(
+        0,
+        chosen[1] + gather(4, 6, row_shift, 1),
+        chosen[0] + gather(4, 6, row_shift, 0),
+        row_shift,
+        lats * WIN - lat * WIN - row_shift,
+    )
+
+    @pl.when(jnp.logical_not(has_up))
+    def _():
+        extra[...] = finish(1, 3, row_shift - WIN)
+
+    ret_out[...] = finish(0, 6, row_shift)
 
     @pl.when(jnp.logical_not(has_up))
     def _():
@@ -451,6 +480,8 @@
             pltpu.VMEM((3, count, width), BF16),
             pltpu.VMEM((2, mates, count, slab), F32),
             pltpu.VMEM((2, mates, count, slab), F32),
+            pltpu.VMEM((2, count, slab), F32),
+            pltpu.VMEM((2, count, model), BF16),
             pltpu.VMEM((3, AREA, slab), BF16),
             pltpu.VMEM((6, AREA, slab), BF16),
             pltpu.VMEM((4, AREA, slab), BF16),

time: 31.2 us -> 30.5 us (0.978)
  Pallas kernels: 29.4 us -> 28.7 us
    pallas_call x1, Pallas kernels: 29.4 us -> 28.7 us  [on_device(): pl.pallas_call(functools.partial(kernel, sizes), out_shape=jax.ShapeDtype...]
where the time goes in v4:
time: 30.5 us; the launch traced here: 30.3 us
  Pallas kernels  28.7 us (94%)
  local copies, waits for them, and re-layouts  1.67 us (5%)
    pallas_call x1, Pallas kernels, on_device(): pl.pallas_call(functools.partial(kernel, sizes), out_shape=jax.ShapeDtype...  28.7 us
    unnamed x1, local copies, waits for them, and re-layouts  1.67 us

profile of v4, /device:TPU:9, one launch (start us, length us, event | category | flops | bytes accessed | tf_op | source)
XLA Modules:
  0.0 30.3 jit_solution(7015307162929221101)
XLA Ops:
  0.0 28.7 %shard_map.82 = bf16[128,1024]{1,0:T(8,128)(2,1)} custom-call(s32[2]{0:T(128)} %off_hbm.1, s32[4,8]{1,0:T(4,128)} %kind_hbm.1, f32[3,8]{1,0:T(4,128)} %bias_hbm.1, f32[1,1024]{1,0:T(1,128)} %bitcast.7, bf16[128,1024]{1,0:T(8,128)(2,1)} %bitcast.5, bf16[128,1024]{1,0:T(8,128)(2,1)} %bitcast.6, bf16[3,1024,512]{2,1,0:T(8,128)(2,1)} %wq_hbm.1, ...), custom_call_target="tpu_custom_call" | custom-call | tf_op jit(solution)/shard_map/pallas_call | solution.py:464
  28.7 1.7 %copy.10 = bf16[8,16,1024]{2,1,0:T(8,128)(2,1)} copy(bf16[8,16,1024]{2,1,0:T(8,128)(2,1)} %bitcast.4) | data formatting | bytes 524288

commit v5 on v4

--- a/solution.py
+++ b/solution.py
@@ -274,7 +274,7 @@
 
         copies = part_copies(turn)
         for step, mate in enumerate(mates):
-            part_out[turn, step] = partial_sum(mate)
+            part_out[turn, step] = partial_sum(mate).astype(BF16)
             copies[step].start()
         part_own[turn] = partial_sum(head)
 
@@ -286,7 +286,7 @@
         d_normed = part_own[turn]
         for step, copy in enumerate(part_copies(turn)):
             copy.wait_recv()
-            d_normed = d_normed + part_in[turn, step]
+            d_normed = d_normed + part_in[turn, step].astype(F32)
         spread = dot(scatter, d_normed.astype(BF16), 1, 0).astype(BF16)
         return spread.reshape(blocks, AREA, slab)
 
@@ -478,8 +478,8 @@
             pltpu.VMEM(w_out.shape, BF16),
             pltpu.VMEM((4, count, width), BF16),
             pltpu.VMEM((3, count, width), BF16),
-            pltpu.VMEM((2, mates, count, slab), F32),
-            pltpu.VMEM((2, mates, count, slab), F32),
+            pltpu.VMEM((2, mates, count, slab), BF16),
+            pltpu.VMEM((2, mates, count, slab), BF16),
             pltpu.VMEM((2, count, slab), F32),
             pltpu.VMEM((2, count, model), BF16),
             pltpu.VMEM((3, AREA, slab), BF16),

time: 30.5 us -> 30.5 us (level)
  no operation moved by 1% of the time
where the time goes in v5:
time: 30.5 us; the launch traced here: 30.3 us
  Pallas kernels  28.7 us (94%)
  local copies, waits for them, and re-layouts  1.67 us (5%)
    pallas_call x1, Pallas kernels, on_device(): pl.pallas_call(functools.partial(kernel, sizes), out_shape=jax.ShapeDtype...  28.7 us
    unnamed x1, local copies, waits for them, and re-layouts  1.67 us

profile of v5, /device:TPU:9, one launch (start us, length us, event | category | flops | bytes accessed | tf_op | source)
XLA Modules:
  0.0 30.3 jit_solution(5920750619745859354)
XLA Ops:
  0.0 28.7 %shard_map.82 = bf16[128,1024]{1,0:T(8,128)(2,1)} custom-call(s32[2]{0:T(128)} %off_hbm.1, s32[4,8]{1,0:T(4,128)} %kind_hbm.1, f32[3,8]{1,0:T(4,128)} %bias_hbm.1, f32[1,1024]{1,0:T(1,128)} %bitcast.7, bf16[128,1024]{1,0:T(8,128)(2,1)} %bitcast.5, bf16[128,1024]{1,0:T(8,128)(2,1)} %bitcast.6, bf16[3,1024,512]{2,1,0:T(8,128)(2,1)} %wq_hbm.1, ...), custom_call_target="tpu_custom_call" | custom-call | tf_op jit(solution)/shard_map/pallas_call | solution.py:464
  28.7 1.7 %copy.10 = bf16[8,16,1024]{2,1,0:T(8,128)(2,1)} copy(bf16[8,16,1024]{2,1,0:T(8,128)(2,1)} %bitcast.4) | data formatting | bytes 524288

commit v6 on v4

--- a/solution.py
+++ b/solution.py
@@ -61,7 +61,6 @@
     part_in,
     part_own,
     chosen,
-    extra,
     ret_out,
     ret_in,
     joined,
@@ -361,15 +360,7 @@
         lats * WIN - lat * WIN - row_shift,
     )
 
-    @pl.when(jnp.logical_not(has_up))
-    def _():
-        extra[...] = finish(1, 3, row_shift - WIN)
-
     ret_out[...] = finish(0, 6, row_shift)
-
-    @pl.when(jnp.logical_not(has_up))
-    def _():
-        ret_out[0:3] = ret_out[0:3] + extra[...]
 
     corner = give_back(5, 0, {"lon": right})
     next_down = give_back(4, 1, {"lat": down})
@@ -380,6 +371,10 @@
     def _():
         corner.start()
         next_down.start()
+
+    @pl.when(jnp.logical_not(has_up))
+    def _():
+        ret_out[0:3] = ret_out[0:3] + finish(1, 3, row_shift - WIN)
 
     aside.start()
 
@@ -482,7 +477,6 @@
             pltpu.VMEM((2, mates, count, slab), F32),
             pltpu.VMEM((2, count, slab), F32),
             pltpu.VMEM((2, count, model), BF16),
-            pltpu.VMEM((3, AREA, slab), BF16),
             pltpu.VMEM((6, AREA, slab), BF16),
             pltpu.VMEM((4, AREA, slab), BF16),
             pltpu.VMEM((heads, count, slab), BF16),

time: 30.5 us -> 30.5 us (level)
  no operation moved by 1% of the time
where the time goes in v6:
time: 30.5 us; the launch traced here: 30.4 us
  Pallas kernels  28.7 us (94%)
  local copies, waits for them, and re-layouts  1.67 us (5%)
    pallas_call x1, Pallas kernels, on_device(): pl.pallas_call(functools.partial(kernel, sizes), out_shape=jax.ShapeDtype...  28.7 us
    unnamed x1, local copies, waits for them, and re-layouts  1.67 us

profile of v6, /device:TPU:9, one launch (start us, length us, event | category | flops | bytes accessed | tf_op | source)
XLA Modules:
  0.0 30.4 jit_solution(14020889479298891182)
XLA Ops:
  0.0 28.7 %shard_map.82 = bf16[128,1024]{1,0:T(8,128)(2,1)} custom-call(s32[2]{0:T(128)} %off_hbm.1, s32[4,8]{1,0:T(4,128)} %kind_hbm.1, f32[3,8]{1,0:T(4,128)} %bias_hbm.1, f32[1,1024]{1,0:T(1,128)} %bitcast.7, bf16[128,1024]{1,0:T(8,128)(2,1)} %bitcast.5, bf16[128,1024]{1,0:T(8,128)(2,1)} %bitcast.6, bf16[3,1024,512]{2,1,0:T(8,128)(2,1)} %wq_hbm.1, ...), custom_call_target="tpu_custom_call" | custom-call | tf_op jit(solution)/shard_map/pallas_call | solution.py:459
  28.7 1.7 %copy.10 = bf16[8,16,1024]{2,1,0:T(8,128)(2,1)} copy(bf16[8,16,1024]{2,1,0:T(8,128)(2,1)} %bitcast.4) | data formatting | bytes 524288
